TPU v7x, 128 devices: a whole 4x4x4 slice. The times are simulated.
128 devices in a mesh: row: 4 (over z_hi, core), col: 32 (over x, y, z_lo).
Axes of the slice: x: 4, y: 4, z: 4 (z_hi: 2, z_lo: 2; z = z_hi * 2 + z_lo), core: 2. Of those that a mesh axis runs over, the one named last changes fastest.
Arguments:
- homolog_embedding: bfloat16 [256, 1024, 256], P('col', 'row'), may hold values from -6 to 6
- pairwise: bfloat16 [1024, 1024, 128], P('row', 'col'), may hold values from -6 to 6
- alignment_mask: int32 [256, 1024], P('col', 'row'), may hold values 0 or 1
- residue_mask: int32 [1024], replicated, may hold values 0 or 1
- query_key_value_gate_matrix: bfloat16 [256, 1024], replicated, may hold values from -0.375 to 0.375
- attend_exit_matrix: bfloat16 [256, 256], replicated, may hold values from -0.375 to 0.375
- bias_weight: float32 [128, 8], replicated, may hold values from -30 to 30
- widen_matrix: bfloat16 [256, 1024], replicated, may hold values from -0.375 to 0.375
- shrink_matrix: bfloat16 [1024, 256], replicated, may hold values from -0.1875 to 0.1875
- left_right_matrix: bfloat16 [256, 64], replicated, may hold values from -0.375 to 0.375
- outer_weight: bfloat16 [1024, 128], replicated, may hold values from -2 to 2
Outputs:
- new_alignment: bfloat16 [256, 1024, 256], P('col', 'row')
- new_pairwise: bfloat16 [1024, 1024, 128], P('row', 'col')
All inputs are finite; a program needn't handle non-finite values. No bound on the sum of `alignment_mask` on one device may be relied on, other than what follows from the above.
Results may differ from a plain program's by a relative error of at most 0.018.
Values may be sent and summed in bfloat16 or wider, within the bound.
A program may use at most 128 MiB of HBM per device.

v0:
```python
import functools

import jax
import jax.numpy as jnp
from jax import lax
from jax.experimental import pallas as pl
from jax.experimental.pallas import tpu as pltpu
from jax.sharding import PartitionSpec as P

MESH = pl.DeviceIdType.MESH
F32 = jnp.float32
BF16 = jnp.bfloat16
EPS = 1e-05
LOG2E = 1.4426950408889634
MASKED = 1000000000.0
COUNT_OFFSET = 0.001
HEADS = 8
NT = (((1,), (1,)), ((), ()))
VMEM_BYTES = 60 * 2**20


def layer_norm(v):
    d = v - jnp.mean(v, -1, keepdims=True)
    return d * lax.rsqrt(jnp.mean(d * d, -1, keepdims=True) + EPS)


class Place:
    def __init__(self):
        self.r = lax.axis_index("row")
        self.c = lax.axis_index("col")
        self.zh, self.core = self.r // 2, lax.rem(self.r, 2)
        self.x, self.y = self.c // 8, lax.rem(self.c // 2, 4)
        self.zl = lax.rem(self.c, 2)
        self.xp, self.xm = lax.rem(self.x + 1, 4), lax.rem(self.x + 3, 4)
        self.yp, self.ym = lax.rem(self.y + 1, 4), lax.rem(self.y + 3, 4)
        self.xo, self.yo = lax.rem(self.x + 2, 4), lax.rem(self.y + 2, 4)

    def along(self, on_x):
        if on_x:
            return [self.at(x=x) for x in (self.xp, self.xm, self.xo)]
        return [self.at(y=y) for y in (self.yp, self.ym, self.yo)]

    def along_with_pair(self, on_x):
        other = 1 - self.zl
        if on_x:
            return self.along(True) + [self.at(x=x, zl=other) for x in (self.x, self.xp, self.xm, self.xo)]
        return self.along(False) + [self.at(y=y, zl=other) for y in (self.y, self.yp, self.ym, self.yo)]

    def at(self, zh=None, core=None, x=None, y=None, zl=None):
        zh = self.zh if zh is None else zh
        core = self.core if core is None else core
        x = self.x if x is None else x
        y = self.y if y is None else y
        zl = self.zl if zl is None else zl
        return (zh * 2 + core, (x * 4 + y) * 2 + zl)


class Sender:
    def __init__(self, send_sems, recv_sems):
        self.send_sems, self.recv_sems, self.copies = send_sems, recv_sems, []

    def start(self, src, dst, device):
        n = len(self.copies)
        copy = pltpu.make_async_remote_copy(
            src_ref=src,
            dst_ref=dst,
            send_sem=self.send_sems.at[n],
            recv_sem=self.recv_sems.at[n],
            device_id=device,
            device_id_type=MESH,
        )
        copy.start()
        self.copies.append(copy)
        return copy

    def wait_sent(self):
        for copy in self.copies:
            copy.wait_send()


class PlaneGather:
    def __init__(self, place, sender, view, x_first):
        self.p, self.s, self.view, self.x_first = place, sender, view, x_first
        self.pending = ()

    def _ring(self, plus, minus):
        p = self.p
        up = p.at(y=p.yp) if self.x_first else p.at(x=p.xp)
        down = p.at(y=p.ym) if self.x_first else p.at(x=p.xm)
        self.pending = (self.s.start(plus, plus, up), self.s.start(minus, minus, down))

    def _wait(self):
        for copy in self.pending:
            copy.wait_recv()

    def first(self, own, devices):
        self.pending = tuple(self.s.start(own, own, device) for device in devices)

    def second(self):
        p = self.p
        self._wait()
        every = slice(0, 4)
        line = self.view(every, p.y) if self.x_first else self.view(p.x, every)
        self._ring(line, line)

    def second_forward(self):
        p = self.p
        self._wait()
        low, high = slice(0, 2), slice(2, 4)
        if self.x_first:
            self._ring(self.view(low, p.ym), self.view(high, p.yp))
        else:
            self._ring(self.view(p.xm, low), self.view(p.xp, high))

    def finish(self):
        self._wait()


def window(index):
    return pl.ds(index.start, index.stop - index.start) if isinstance(index, slice) else index


def greet(devices):
    barrier = pltpu.get_barrier_semaphore()
    for device in devices:
        pl.semaphore_signal(barrier, inc=1, device_id=device, device_id_type=MESH)
    return barrier


def fold_max(v):
    parts = [v[8 * i : 8 * i + 8] for i in range(v.shape[0] // 8)]
    while len(parts) > 1:
        parts = [
            jnp.maximum(parts[i], parts[i + 1]) if i + 1 < len(parts) else parts[i]
            for i in range(0, len(parts), 2)
        ]
    return parts[0]


def attention_kernel(
    x_ref, pair_ref, mask_ref, w_ref, bw_ref,
    out_ref,
    pair32, stage, bias, xg, maskg, maskb, kt, vt, qt, gate, att,
    s0, s1, s2, s3, send_sems, recv_sems,
):
    p = Place()
    peers = p.along(True) + p.along(False) + [p.at(zl=1 - p.zl), p.at(core=1 - p.core), p.at(zh=1 - p.zh)]
    barrier = greet(peers)
    sender = Sender(send_sems, recv_sems)

    pair32[...] = pair_ref[...].astype(F32)
    bw = bw_ref[...] * LOG2E
    bw_high = bw.astype(BF16)
    bw_low = (bw - bw_high.astype(F32)).astype(BF16)
    bw_rows = jnp.concatenate([bw_high, bw_low], 0)
    bw_both = jnp.concatenate([bw_rows, bw_rows], 1)

    @pl.loop(0, 8)
    def _(jb):
        for u in range(4):
            j = jb * 4 + u
            n = layer_norm(pair32[pl.ds(j, 256, stride=32), :])
            high = n.astype(BF16)
            low = (n - high.astype(F32)).astype(BF16)
            both = jnp.concatenate([high, low], 1)
            r = lax.dot_general(bw_both, both, NT, preferred_element_type=F32)
            r = r[:8] + r[8:]
            for t in range(2):
                stage[t, pl.ds(j, 8, stride=32), :] = r[:, t * 128 : t * 128 + 128]

    for h in range(HEADS):
        rows = slice(h * 32, h * 32 + 32)
        bias[h, p.x, p.y, pl.ds(p.zl * 32, 32), :] = jnp.concatenate([stage[0, rows, :], stage[1, rows, :]], 1)
    pl.semaphore_wait(barrier, len(peers))

    z_copies = {}

    def to_pair(k):
        for h in (2 * k, 2 * k + 1):
            own = bias.at[h, p.x, p.y, pl.ds(p.zl * 32, 32)]
            z_copies[h] = sender.start(own, own, p.at(zl=1 - p.zl))

    to_pair(0)

    def head_view(h):
        return lambda x, y: bias.at[h, window(x), window(y)]

    gathers = [PlaneGather(p, sender, head_view(h), h % 2 == 0) for h in range(HEADS)]

    def first(k):
        for h in (2 * k, 2 * k + 1):
            z_copies[h].wait_recv()
            gathers[h].first(bias.at[h, p.x, p.y], p.along(h % 2 == 0))

    def second(k):
        for h in (2 * k, 2 * k + 1):
            gathers[h].second()

    def second_forward(k):
        for h in (2 * k, 2 * k + 1):
            gathers[h].second_forward()

    def finish(k):
        for h in (2 * k, 2 * k + 1):
            gathers[h].finish()

    def normalise(s):
        xg[s, p.r] = layer_norm(x_ref[s].astype(F32)).astype(BF16)

    core_peer, z_peer = p.at(core=1 - p.core), p.at(zh=1 - p.zh)
    far = (1 - p.zh) * 2 + p.core
    near_copies, far_copies, pass_copies = [], [], []

    def share(g):
        own = xg.at[pl.ds(2 * g, 2), p.r]
        far_copies.append(sender.start(own, own, z_peer))
        near_copies.append(sender.start(own, own, core_peer))

    wq = w_ref[:, 0:256]
    wk = w_ref[:, 256:512]
    wv = w_ref[:, 512:768]
    wg = w_ref[:, 768:1024]
    wq_t = jnp.transpose(wq.astype(F32)).astype(BF16)
    wv_t = jnp.transpose(wv.astype(F32)).astype(BF16)

    def project(s):
        own = xg[s, p.r]
        q = lax.dot_general(wq_t, own, NT, preferred_element_type=F32)
        qt[s] = (q * (LOG2E * 32**-0.5)).astype(BF16)
        gate[s] = jax.nn.sigmoid(jnp.dot(own, wg, preferred_element_type=F32))

    for s in range(4):
        normalise(s)
    first(0)
    to_pair(1)
    for s in range(4, 8):
        normalise(s)
    share(0)
    maskg[p.r] = (mask_ref[...].astype(F32) - 1.0) * (MASKED * LOG2E)
    mask_copies = [
        sender.start(maskg.at[p.r], maskg.at[p.r], core_peer),
        sender.start(maskg.at[p.r], maskg.at[p.r], z_peer),
    ]
    for s in range(4):
        project(s)
    second(0)
    first(1)
    to_pair(2)
    to_pair(3)
    share(1)
    for s in range(4, 8):
        project(s)
    first(2)
    second(1)
    for copy in mask_copies:
        copy.wait_recv()
    mask_copies.append(sender.start(maskg.at[far], maskg.at[far], core_peer))
    mask_copies[2].wait_recv()
    for r in range(4):
        columns = jnp.transpose(maskg[r])
        for s in range(8):
            maskb[s, r * 256 : r * 256 + 256, :] = jnp.broadcast_to(columns[:, s : s + 1], (256, 128))

    vt[:, :, 32:48, :] = jnp.ones((8, 8, 16, 1024), BF16)
    def pass_on(g):
        far_copies[g].wait_recv()
        piece = xg.at[pl.ds(2 * g, 2), far]
        pass_copies.append(sender.start(piece, piece, core_peer))

    def project_all(g):
        near_copies[g].wait_recv()
        pass_copies[g].wait_recv()

        @pl.loop(2 * g, 2 * g + 2)
        def _(s):
            for r in range(4):
                rows = xg[s, r]
                k = jnp.dot(rows, wk, preferred_element_type=F32).astype(BF16)
                kt[s, 0, r * 256 : r * 256 + 256, :] = k[:, :128]
                kt[s, 1, r * 256 : r * 256 + 256, :] = k[:, 128:]
                v = lax.dot_general(wv_t, rows, NT, preferred_element_type=F32).astype(BF16)
                vt[s, :, 0:32, r * 256 : r * 256 + 256] = v.reshape(8, 32, 256)

    head_of = lax.broadcasted_iota(jnp.int32, (128, 256), 0) // 32

    def step(new, new_scores, now, now_scores, now_max):
        new_max, total = [None, None], [None, None]
        if new is not None:
            h, first = new
            tile = h // 4
            q = [
                jnp.where(
                    head_of == h % 4, qt[first + u, tile * 128 : tile * 128 + 128, :].astype(F32), 0.0
                ).astype(BF16)
                for u in range(2)
            ]
        for jc in range(4):
            rows = slice(jc * 256, jc * 256 + 256)
            if new is not None:
                b = bias[h, jc].reshape(256, 256)
                for u in range(2):
                    m = maskb[first + u, rows, :]
                    sc = jnp.dot(kt[first + u, tile, rows, :], q[u], preferred_element_type=F32)
                    sc = sc + b + jnp.concatenate([m, m], 1)
                    new_scores[u][rows, :] = sc
                    f = fold_max(sc)
                    new_max[u] = f if new_max[u] is None else jnp.maximum(new_max[u], f)
            if now is not None:
                hn, start = now
                for u in range(2):
                    e = jnp.exp2(now_scores[u][rows, :] - now_max[u]).astype(BF16)
                    a = jnp.dot(vt[start + u, hn, :, rows], e, preferred_element_type=F32)
                    total[u] = a if total[u] is None else total[u] + a
        if now is not None:
            for u in range(2):
                att[start + u, hn * 32 : hn * 32 + 32, :] = total[u][:32] / total[u][32:33]
        if new is not None:
            return tuple(jnp.max(m, axis=0, keepdims=True) for m in new_max)

    sets = ((s0, s1), (s2, s3))
    last = [None, None, 0]

    def attend_to(*items):
        for new in items:
            now, top, n = last
            number = n + 1
            scores = sets[number % 2]
            last[:] = new, step(new, scores, now, sets[n % 2], top), number

    second_forward(0)
    second(2)
    first(3)
    pass_on(0)
    share(2)
    pass_on(1)
    project_all(0)
    share(3)
    pass_on(2)
    project_all(1)
    second_forward(1)
    second(3)
    finish(0)
    pass_on(3)
    attend_to((0, 0), (0, 2), (1, 0), (1, 2))
    project_all(2)
    attend_to((0, 4), (1, 4))
    project_all(3)
    second_forward(2)
    attend_to((0, 6), (1, 6))
    finish(1)
    attend_to((2, 0), (2, 2), (2, 4), (2, 6))
    second_forward(3)
    attend_to((3, 0), (3, 2), (3, 4), (3, 6))
    for k in (2, 3):
        finish(k)
        attend_to(*((h, 2 * g) for h in (2 * k, 2 * k + 1) for g in range(4)))
    step(None, None, last[0], sets[last[2] % 2], last[1])

    for s in range(8):
        out_ref[s] = (jnp.transpose(att[s]) * gate[s]).astype(BF16)
    sender.wait_sent()


def transition_kernel(
    x_ref, gated_ref, pair_ref, mask_ref, res_ref, wo_ref, w1_ref, w2_ref, wlr_ref, ow_ref,
    align_ref, out_ref,
    lscr, rscr, raw, left, maskall, rsend, rrecv, rt, obuf, upd, counts, col_scr,
    send_sems, recv_sems, r_send_sems, r_recv_sems, pass_sems,
):
    p = Place()
    home = p.c // 8
    core_peer = p.at(core=1 - p.core)
    receives = lax.rem(home, 2) == p.core
    greeted = p.along_with_pair(True) + p.along_with_pair(False) + [core_peer]
    barrier = greet(greeted)

    @pl.loop(0, 32)
    def _(c):
        @pl.when(jnp.logical_and(receives, jnp.logical_or(home != p.r, c != p.c)))
        def _():
            pl.semaphore_signal(barrier, inc=1, device_id=(home, c), device_id_type=MESH)

    sender = Sender(send_sems, recv_sems)
    mask = mask_ref[...].astype(F32)

    wl_t = wlr_ref[0:32, :]
    wr = wlr_ref[32:64, :]
    wr4 = jnp.concatenate([wr, wr, wr, wr], 0)
    mask_cols = jnp.transpose(mask)

    def transition_block(t, q):
        half = slice(t * 128, t * 128 + 128)
        four = slice(4 * q, 4 * q + 4)
        rows = x_ref[four, half, :].reshape(512, 256).astype(F32)
        gated = gated_ref[four, half, :].reshape(512, 256)
        after = rows + jnp.dot(gated, wo_ref[...], preferred_element_type=F32)
        hidden = jnp.dot(layer_norm(after).astype(BF16), w1_ref[...], preferred_element_type=F32)
        hidden = jnp.maximum(hidden, 0.0).astype(BF16)
        after = after + jnp.dot(hidden, w2_ref[...], preferred_element_type=F32)
        align_ref[four, half, :] = after.astype(BF16).reshape(4, 128, 256)
        n = layer_norm(after).astype(BF16)
        l = lax.dot_general(wl_t, n, NT, preferred_element_type=F32)
        rr = lax.dot_general(n, wr4, NT, preferred_element_type=F32)
        for u in range(4):
            s = 4 * q + u
            cols = slice(u * 128, u * 128 + 128)
            lscr[t, s * 32 : s * 32 + 32, :] = l[:, cols] * mask[s : s + 1, half]
            start = s * 256 + t * 128
            rscr[start : start + 128, :] = rr[cols] * mask_cols[half, s : s + 1]

    def own_left(t, a):
        return lscr[t, pl.ds(a, 8, stride=32), :]

    def fill_left(t):
        for a in range(16):
            both = jnp.concatenate([own_left(t, a), own_left(t, a + 16)], 0)
            raw[t, p.x, p.y, p.zl, :, a * 128 : a * 128 + 128] = both.astype(BF16)

    def left_part(t, part):
        lanes = pl.ds(part * 1024, 1024)
        view = lambda x, y: raw.at[t, window(x), window(y), pl.ds(0, 2), pl.ds(0, 16), lanes]
        own = raw.at[t, p.x, p.y, p.zl, pl.ds(0, 16), lanes]
        return PlaneGather(p, sender, view, part == 0), own, p.along_with_pair(part == 0)

    def mask_view(x, y):
        return maskall.at[window(x), window(y), pl.ds(0, 2), pl.ds(0, 16)]

    mask_unit = (
        PlaneGather(p, sender, mask_view, False),
        maskall.at[p.x, p.y, p.zl, pl.ds(0, 16)],
        p.along_with_pair(False),
    )
    halves = [[left_part(0, 0), left_part(0, 1), mask_unit], [left_part(1, 0), left_part(1, 1)]]

    def first(t):
        for unit, own, devices in halves[t]:
            unit.first(own, devices)

    def second(t):
        for unit, _, _ in halves[t]:
            unit.second()

    def second_forward(t):
        for unit, _, _ in halves[t]:
            unit.second_forward()

    def finish(t):
        for unit, _, _ in halves[t]:
            unit.finish()

    lane = lax.broadcasted_iota(jnp.int32, (8, 128), 1) // 32

    def right_copy(k, zh):
        return pltpu.make_async_remote_copy(
            src_ref=rsend.at[k],
            dst_ref=rrecv.at[p.c],
            send_sem=r_send_sems.at[k * 2 + zh],
            recv_sem=r_recv_sems.at[p.c],
            device_id=(zh * 2 + p.core, p.r * 8 + k),
            device_id_type=MESH,
        )

    def is_remote(k, zh):
        return jnp.logical_or(p.c != p.r * 8 + k, p.zh != zh)

    def send_right(t):
        for k in range(4 * t, 4 * t + 4):
            rows = []
            for half in range(2):
                parts = []
                for q in range(4):
                    j = k * 32 + half * 16 + q * 4
                    v = [rscr[pl.ds(j + u, 8, stride=256), :] for u in range(4)]
                    parts.append(
                        jnp.where(lane == 0, v[0], jnp.where(lane == 1, v[1], jnp.where(lane == 2, v[2], v[3])))
                    )
                parts.append(mask[:, t * 128 : t * 128 + 128])
                rows.append(jnp.concatenate(parts, 1))
            rsend[k] = jnp.concatenate(rows, 0).astype(BF16)

        @pl.loop(0, 8)
        def _(n):
            k, zh = 4 * t + n // 2, lax.rem(n, 2)

            @pl.when(is_remote(k, zh))
            def _():
                right_copy(k, zh).start()

            @pl.when(jnp.logical_not(is_remote(k, zh)))
            def _():
                pltpu.make_async_copy(rsend.at[k], rrecv.at[p.c], r_recv_sems.at[p.c]).start()

    right_pass = pltpu.make_async_remote_copy(
        src_ref=rrecv,
        dst_ref=rrecv,
        send_sem=pass_sems.at[0],
        recv_sem=pass_sems.at[1],
        device_id=core_peer,
        device_id_type=MESH,
    )

    transition_block(0, 0)
    transition_block(0, 1)
    fill_left(0)
    maskall[p.x, p.y, p.zl] = jnp.concatenate([mask, mask], 0).astype(BF16)
    pl.semaphore_wait(barrier, len(greeted) + 16 - (home == p.r).astype(jnp.int32))
    first(0)
    send_right(0)
    transition_block(1, 0)
    transition_block(1, 1)
    fill_left(1)
    second(0)
    first(1)
    send_right(1)
    ow_t = jnp.transpose(ow_ref[...].astype(F32)).astype(BF16)
    second_forward(0)
    second(1)

    @pl.when(receives)
    def _():
        @pl.loop(0, 32)
        def _(c):
            pltpu.make_async_copy(rrecv.at[c], rrecv.at[c], r_recv_sems.at[c]).wait()

        right_pass.start()

    @pl.when(jnp.logical_not(receives))
    def _():
        right_pass.wait_recv()

    place_in_tile = pl.multiple_of(lax.rem(p.c, 4) * 32, 32)
    for half in range(2):
        rows = rrecv[:, :, :].astype(F32)[:, half * 8 : half * 8 + 8, :].reshape(256, 640)
        rt[half * 512 : half * 512 + 512, :] = jnp.transpose(rows[:, :512]).astype(BF16)
        if half == 0:
            col_scr[...] = jnp.transpose(rows[:, 512:])
    mask_j = col_scr[pl.ds(place_in_tile, 32), :].astype(BF16)
    res = res_ref[...].astype(F32)
    rowid = lax.broadcasted_iota(jnp.int32, (8, 128), 0)
    pick = lambda n: jnp.sum(jnp.where(rowid == n, res, 0.0), 0, keepdims=True)
    res_i = jnp.concatenate([pick(p.r * 2), pick(p.r * 2 + 1)], 1)
    res_j = jnp.transpose(jnp.broadcast_to(pick(p.c // 4), (128, 128)))
    col_scr[:, 0:128] = res_j
    res_j = col_scr[pl.ds(place_in_tile, 32), 0:128]

    for t in range(2):
        finish(t)
        if t == 0:
            mask_i = maskall[...].astype(F32)[:, :, :, :8, :].reshape(256, 256).astype(BF16)
            pair_count = jnp.dot(mask_j, mask_i, preferred_element_type=F32) + COUNT_OFFSET
            factor = jnp.concatenate([res_j, res_j], 1) * res_i / pair_count
            counts[0] = factor[:, :128]
            counts[1] = factor[:, 128:]

        @pl.loop(0, 16)
        def _(n):
            x, y = n // 4, lax.rem(n, 4)
            two = raw[t, x, y].astype(F32)
            rows = pl.ds(pl.multiple_of(n * 16, 16), 16)
            for part in range(2):
                both = two[:, part * 8 : part * 8 + 8, :].reshape(16, 2048)
                left[rows, part * 2048 : part * 2048 + 2048] = both.astype(BF16)

        @pl.loop(0, 4)
        def _(n):
            for u in range(4):
                pair = n * 4 + u
                lanes = pl.ds(pl.multiple_of(pair * 256, 256), 256)
                o = jnp.dot(rt[...], left[:, lanes], preferred_element_type=F32).astype(BF16)
                for v in range(2):
                    obuf[:, pair * 2 + v] = o[:, v * 128 : v * 128 + 128].reshape(32, 32, 128)

        if t == 0:
            second_forward(1)

        @pl.loop(0, 4)
        def _(n):
            for u in range(4):
                j = n * 8 + u * 2
                two = jnp.concatenate([obuf[j + v].reshape(1024, 128) for v in range(2)], 1)
                o = jnp.dot(ow_t, two, preferred_element_type=F32)
                for v in range(2):
                    scale = counts[t, pl.ds(j + v, 1), :]
                    upd[pl.ds(t * 4096 + j + v, 128, stride=32), :] = jnp.transpose(o[:, v * 128 : v * 128 + 128] * scale)

        @pl.loop(0, 4)
        def _(n):
            rows = pl.ds(pl.multiple_of(t * 4096 + n * 1024, 1024), 1024)
            out_ref[rows, :] = (pair_ref[rows, :].astype(F32) + upd[rows, :]).astype(BF16)

    sender.wait_sent()

    @pl.when(receives)
    def _():
        right_pass.wait_send()

    @pl.loop(0, 16)
    def _(n):
        k, zh = n // 2, lax.rem(n, 2)

        @pl.when(is_remote(k, zh))
        def _():
            right_copy(k, zh).wait_send()


def vmem(n):
    return [pl.BlockSpec(memory_space=pltpu.VMEM)] * n


def attend(x, pair, mask, w, bw):
    copies = 8 + 3 + 12 + 8 * 7
    return pl.pallas_call(
        attention_kernel,
        out_shape=jax.ShapeDtypeStruct((8, 256, 256), BF16),
        in_specs=vmem(5),
        out_specs=pl.BlockSpec(memory_space=pltpu.VMEM),
        scratch_shapes=[
            pltpu.VMEM((8192, 128), F32),
            pltpu.VMEM((2, 256, 128), F32),
            pltpu.VMEM((8, 4, 4, 64, 256), F32),
            pltpu.VMEM((8, 4, 256, 256), BF16),
            pltpu.VMEM((4, 8, 256), F32),
            pltpu.VMEM((8, 1024, 128), F32),
            pltpu.VMEM((8, 2, 1024, 128), BF16),
            pltpu.VMEM((8, 8, 48, 1024), BF16),
            pltpu.VMEM((8, 256, 256), BF16),
            pltpu.VMEM((8, 256, 256), F32),
            pltpu.VMEM((8, 256, 256), F32),
        ]
        + [pltpu.VMEM((1024, 256), F32)] * 4
        + [pltpu.SemaphoreType.DMA((copies,)), pltpu.SemaphoreType.DMA((copies,))],
        compiler_params=pltpu.CompilerParams(collective_id=0, has_side_effects=True, vmem_limit_bytes=VMEM_BYTES),
    )(x, pair, mask, w, bw)


def transition(x, gated, pair, mask, res, wo, w1, w2, wlr, ow):
    copies = 5 * 11
    return pl.pallas_call(
        transition_kernel,
        out_shape=(
            jax.ShapeDtypeStruct((8, 256, 256), BF16),
            jax.ShapeDtypeStruct((8192, 128), BF16),
        ),
        in_specs=vmem(10),
        out_specs=tuple(vmem(2)),
        scratch_shapes=[
            pltpu.VMEM((2, 256, 128), F32),
            pltpu.VMEM((2048, 128), F32),
            pltpu.VMEM((2, 4, 4, 2, 16, 2048), BF16),
            pltpu.VMEM((256, 4096), BF16),
            pltpu.VMEM((4, 4, 2, 16, 256), BF16),
            pltpu.VMEM((8, 16, 640), BF16),
            pltpu.VMEM((32, 16, 640), BF16),
            pltpu.VMEM((1024, 256), BF16),
            pltpu.VMEM((32, 32, 32, 128), BF16),
            pltpu.VMEM((8192, 128), F32),
            pltpu.VMEM((2, 32, 128), F32),
            pltpu.VMEM((128, 256), F32),
            pltpu.SemaphoreType.DMA((copies,)),
            pltpu.SemaphoreType.DMA((copies,)),
            pltpu.SemaphoreType.DMA((16,)),
            pltpu.SemaphoreType.DMA((32,)),
            pltpu.SemaphoreType.DMA((2,)),
        ],
        compiler_params=pltpu.CompilerParams(collective_id=1, has_side_effects=True, vmem_limit_bytes=VMEM_BYTES),
    )(x, gated, pair, mask, res, wo, w1, w2, wlr, ow)


def per_device(x, pairwise, mask, residue_mask, w, wo, bw, w1, w2, wlr, ow):
    pair = pairwise.reshape(8192, 128)
    gated = attend(x, pair, mask, w, bw.T)
    alignment, new_pair = transition(x, gated, pair, mask, residue_mask.reshape(8, 128), wo, w1, w2, wlr.T, ow)
    return alignment, new_pair.reshape(256, 32, 128)


def solution(mesh):
    return jax.shard_map(
        per_device,
        mesh=mesh,
        in_specs=(P("col", "row", None), P("row", "col", None), P("col", "row")) + (P(),) * 8,
        out_specs=(P("col", "row", None), P("row", "col", None)),
        check_vma=False,
    )
```

profile of v0, /device:TPU:1, one launch (start us, length us, event | category | flops | bytes accessed | tf_op | source)
XLA Modules:
  0.0 135.5 jit_solution(13729660267520865859)
XLA Ops:
  0.6 71.6 %shard_map.122.gated_ref = bf16[8,256,256]{2,1,0:T(8,128)(2,1)} custom-call(bf16[8,256,256]{2,1,0:T(8,128)(2,1)} %x_ref.3, bf16[8192,128]{1,0:T(8,128)(2,1)} %bitcast.5, s32[8,256]{1,0:T(8,128)} %mask_ref.3, bf16[256,1024]{1,0:T(8,128)(2,1)} %w_ref.1, f32[8,128]{1,0:T(8,128)} %bitcast.10), custom_call_target="tpu_custom_call" | custom-call | tf_op jit(solution)/shard_map/pallas_call | solution.py:612
  72.2 59.5 %shard_map.123 = (bf16[8,256,256]{2,1,0:T(8,128)(2,1)}, bf16[8192,128]{1,0:T(8,128)(2,1)}) custom-call(bf16[8,256,256]{2,1,0:T(8,128)(2,1)} %x_ref.3, bf16[8,256,256]{2,1,0:T(8,128)(2,1)} %shard_map.122.gated_ref, bf16[8192,128]{1,0:T(8,128)(2,1)} %bitcast.6, s32[8,256]{1,0:T(8,128)} %mask_ref.3, s32[8,128]{1,0:T(8,128)} %bitcast.9, ...), custom_call_target="tpu_custom_call" | custom-call | tf_op jit(solution)/shard_map/pallas_call | solution.py:638
  131.7 0.0 copy-start
  131.8 2.4 %copy.15 = bf16[8,256,256]{2,1,0:T(8,128)(2,1)} copy(bf16[8,256,256]{2,1,0:T(8,128)(2,1)} %get-tuple-element.8) | data formatting | bytes 2097152
  134.2 0.0 copy-done
  134.2 1.3 copy.16
Async XLA Ops:
  131.7 2.4 %copy-start = (bf16[8192,128]{1,0:T(8,128)(2,1)S(1)}, bf16[8192,128]{1,0:T(8,128)(2,1)}, u32[]{:S(2)}) copy-start(bf16[8192,128]{1,0:T(8,128)(2,1)} %get-tuple-element.5) | copy-start | bytes 6291460
where the time goes:
time: 136 us; the launch traced here: 135 us
  Pallas kernels  131 us (96%)
  local copies, waits for them, and re-layouts  3.73 us (3%)
    pallas_call x1, Pallas kernels, attend(): pl.pallas_call(attention_kernel, out_shape=jax.ShapeDtypeStruct((8, 256,...  71.6 us
    pallas_call x1, Pallas kernels, transition(): pl.pallas_call(transition_kernel, out_shape=(jax.ShapeDtypeStruct((8, 256...  59.5 us
    unnamed x4, local copies, waits for them, and re-layouts  3.73 us

commit v1 on v0

--- a/solution.py
+++ b/solution.py
@@ -561,10 +561,10 @@
                 both = two[:, part * 8 : part * 8 + 8, :].reshape(16, 2048)
                 left[rows, part * 2048 : part * 2048 + 2048] = both.astype(BF16)
 
-        @pl.loop(0, 4)
+        @pl.loop(0, 2)
         def _(n):
-            for u in range(4):
-                pair = n * 4 + u
+            for u in range(8):
+                pair = n * 8 + u
                 lanes = pl.ds(pl.multiple_of(pair * 256, 256), 256)
                 o = jnp.dot(rt[...], left[:, lanes], preferred_element_type=F32).astype(BF16)
                 for v in range(2):
@@ -573,10 +573,10 @@
         if t == 0:
             second_forward(1)
 
-        @pl.loop(0, 4)
+        @pl.loop(0, 2)
         def _(n):
-            for u in range(4):
-                j = n * 8 + u * 2
+            for u in range(8):
+                j = n * 16 + u * 2
                 two = jnp.concatenate([obuf[j + v].reshape(1024, 128) for v in range(2)], 1)
                 o = jnp.dot(ow_t, two, preferred_element_type=F32)
                 for v in range(2):

time: 136 us -> 135 us (level)
  no operation moved by 1% of the time
where the time goes in v1:
time: 135 us
  Pallas kernels  130 us (96%)
  local copies, waits for them, and re-layouts  3.73 us (3%)
    pallas_call x1, Pallas kernels, attend(): pl.pallas_call(attention_kernel, out_shape=jax.ShapeDtypeStruct((8, 256,...  71.6 us
    pallas_call x1, Pallas kernels, transition(): pl.pallas_call(transition_kernel, out_shape=(jax.ShapeDtypeStruct((8, 256...  58.7 us
    unnamed x4, local copies, waits for them, and re-layouts  3.73 us

profile of v1, /device:TPU:1, one launch (start us, length us, event | category | flops | bytes accessed | tf_op | source)
XLA Modules:
  0.0 134.7 jit_solution(10062080187399196479)
XLA Ops:
  0.6 71.6 %shard_map.122.gated_ref = bf16[8,256,256]{2,1,0:T(8,128)(2,1)} custom-call(bf16[8,256,256]{2,1,0:T(8,128)(2,1)} %x_ref.3, bf16[8192,128]{1,0:T(8,128)(2,1)} %bitcast.5, s32[8,256]{1,0:T(8,128)} %mask_ref.3, bf16[256,1024]{1,0:T(8,128)(2,1)} %w_ref.1, f32[8,128]{1,0:T(8,128)} %bitcast.10), custom_call_target="tpu_custom_call" | custom-call | tf_op jit(solution)/shard_map/pallas_call | solution.py:612
  72.2 58.7 %shard_map.123 = (bf16[8,256,256]{2,1,0:T(8,128)(2,1)}, bf16[8192,128]{1,0:T(8,128)(2,1)}) custom-call(bf16[8,256,256]{2,1,0:T(8,128)(2,1)} %x_ref.3, bf16[8,256,256]{2,1,0:T(8,128)(2,1)} %shard_map.122.gated_ref, bf16[8192,128]{1,0:T(8,128)(2,1)} %bitcast.6, s32[8,256]{1,0:T(8,128)} %mask_ref.3, s32[8,128]{1,0:T(8,128)} %bitcast.9, ...), custom_call_target="tpu_custom_call" | custom-call | tf_op jit(solution)/shard_map/pallas_call | solution.py:638
  131.0 0.0 copy-start
  131.0 2.4 %copy.15 = bf16[8,256,256]{2,1,0:T(8,128)(2,1)} copy(bf16[8,256,256]{2,1,0:T(8,128)(2,1)} %get-tuple-element.8) | data formatting | bytes 2097152
  133.4 0.0 copy-done
  133.4 1.3 copy.16
Async XLA Ops:
  131.0 2.4 %copy-start = (bf16[8192,128]{1,0:T(8,128)(2,1)S(1)}, bf16[8192,128]{1,0:T(8,128)(2,1)}, u32[]{:S(2)}) copy-start(bf16[8192,128]{1,0:T(8,128)(2,1)} %get-tuple-element.5) | copy-start | bytes 6291460
